TPU v7x, 128 devices: a whole 4x4x4 slice. The times are simulated.
128 devices in a mesh: row: 8 (over y, x_lo), col: 16 (over x_hi, z, core).
Axes of the slice: x: 4 (x_hi: 2, x_lo: 2; x = x_hi * 2 + x_lo), y: 4, z: 4, core: 2. Of those that a mesh axis runs over, the one named last changes fastest.
Arguments:
- pair_rep: bfloat16 [1536, 1536, 128], P('row', 'col'), may hold values from -6 to 6
- res_mask: int32 [1536], replicated, may hold values 0 or 1
- norm_gain: float32 [128], replicated, may hold values from 0.1 to 1.9
- norm_bias: float32 [128], replicated, may hold values from -3 to 3
- w_left: bfloat16 [128, 128], replicated, may hold values from -0.5 to 0.5
- w_left_gate: bfloat16 [128, 128], replicated, may hold values from -0.5 to 0.5
- w_right: bfloat16 [128, 128], replicated, may hold values from -0.5 to 0.5
- w_right_gate: bfloat16 [128, 128], replicated, may hold values from -0.5 to 0.5
- w_out_gate: bfloat16 [128, 128], replicated, may hold values from -0.5 to 0.5
- out_gain: float32 [128], replicated, may hold values from 0.1 to 1.9
- out_bias: float32 [128], replicated, may hold values from -3 to 3
- w_out: bfloat16 [128, 128], replicated, may hold values from -0.5 to 0.5
Outputs:
- update_t: bfloat16 [1536, 1536, 128], P('col', 'row')
All inputs are finite; a program needn't handle non-finite values.
Results may differ from a plain program's by a relative error of at most 0.0059.
Values may be sent and summed in bfloat16 or wider, within the bound.
A program may use at most 128 MiB of HBM per device.

v0:
```python
import jax
import jax.numpy as jnp
from jax import lax
from jax.sharding import PartitionSpec as P

EPS = 1e-05


def norm_last(values, gain, bias):
    mean = jnp.mean(values, axis=-1, keepdims=True)
    centred = values - mean
    var = jnp.mean(centred * centred, axis=-1, keepdims=True)
    return centred * lax.rsqrt(var + EPS) * gain + bias


def on_device(
    pair_rep,
    res_mask,
    norm_gain,
    norm_bias,
    w_left,
    w_left_gate,
    w_right,
    w_right_gate,
    w_out_gate,
    out_gain,
    out_bias,
    w_out,
):
    rows_here, cols_here, _ = pair_rep.shape
    mask_f = res_mask.astype(jnp.float32)
    row_mask = lax.dynamic_slice_in_dim(mask_f, lax.axis_index("row") * rows_here, rows_here)
    col_mask = lax.dynamic_slice_in_dim(mask_f, lax.axis_index("col") * cols_here, cols_here)
    pmask = row_mask[:, None] * col_mask[None, :]
    normed = norm_last(pair_rep.astype(jnp.float32), norm_gain, norm_bias).astype(jnp.bfloat16)

    def project(w_value, w_gate):
        value = jnp.einsum("ikd,dc->cik", normed, w_value, preferred_element_type=jnp.float32)
        gate = jnp.einsum("ikd,dc->cik", normed, w_gate, preferred_element_type=jnp.float32)
        return (jax.nn.sigmoid(gate) * value * pmask[None]).astype(jnp.bfloat16)

    stacked = jnp.stack([project(w_left, w_left_gate), project(w_right, w_right_gate)])
    edges = lax.all_to_all(
        lax.all_to_all(stacked, "row", split_axis=1, concat_axis=2, tiled=True),
        "col",
        split_axis=1,
        concat_axis=3,
        tiled=True,
    )
    product = jnp.einsum(
        "cjk,cik->cji", edges[1], edges[0], preferred_element_type=jnp.float32
    ).astype(jnp.bfloat16)
    by_cols = lax.all_to_all(product, "col", split_axis=1, concat_axis=0, tiled=True)
    gathered = lax.all_to_all(by_cols, "row", split_axis=2, concat_axis=0, tiled=True)
    block = gathered.astype(jnp.float32)
    mean = jnp.mean(block, axis=0, keepdims=True)
    centred = block - mean
    var = jnp.mean(centred * centred, axis=0, keepdims=True)
    tnorm = (
        centred * lax.rsqrt(var + EPS) * out_gain[:, None, None] + out_bias[:, None, None]
    ).astype(jnp.bfloat16)
    proj = jnp.einsum("cji,cd->jid", tnorm, w_out, preferred_element_type=jnp.float32)
    gate = jnp.einsum("ijc,cd->jid", normed, w_out_gate, preferred_element_type=jnp.float32)
    return (jax.nn.sigmoid(gate) * proj).astype(jnp.bfloat16)


def solution(mesh):
    placed = (P("row", "col", None), P(), P(), P(), P(), P(), P(), P(), P(), P(), P(), P())
    return jax.shard_map(
        on_device, mesh=mesh, in_specs=placed, out_specs=P("col", "row", None), check_vma=False
    )
```

profile of v0, /device:TPU:1, one launch (start us, length us, event | category | flops | bytes accessed | tf_op | source)
XLA Modules:
  0.0 724.2 jit_solution(2399057011369235636)
XLA Ops:
  0.0 0.7 convert_element_type.47
  0.7 0.1 dynamic_slice.6
  0.8 0.1 dynamic_slice.7
  0.9 4.3 convert_reduce_fusion
  5.2 7.6 %fusion.6 = f32[192,96]{1,0:T(8,128)S(1)} fusion(bf16[192,96,128]{2,1,0:T(8,128)(2,1)} %param.12, f32[192,96]{1,0:T(8,128)S(1)} %broadcast_multiply_fusion.2), kind=kLoop, calls=%fused_computation.10 | loop fusion | flops 9418752 | bytes 4866048 | tf_op jit(solution)/shard_map/reduce_sum | solution.py:12
  12.8 0.1 add_rsqrt_fusion.1
  12.9 0.0 copy-done
  12.9 0.0 copy-done.7
  12.9 0.0 copy-done.6
  12.9 0.0 copy-done.2
  13.0 0.0 copy-start.4
  13.0 5.1 fusion.19
  18.0 0.0 copy-done.4
  18.1 5.1 fusion.16
  23.1 10.8 %fusion.12 = bf16[1,128,192,96]{1,3,2,0:T(8,128)(2,1)} fusion(f32[192,96]{1,0:T(8,128)S(1)} %get-tuple-element.6, f32[192,96,128]{2,1,0:T(8,128)S(1)} %fusion.19, bf16[128,128]{1,0:T(8,128)(2,1)S(1)} %copy-done.10, bf16[192,96,128]{2,1,0:T(8,128)(2,1)S(1)} %copy-done.2, f32[128]{0:T(128)S(1)} %copy-done.6, f32[128]{0:T(128)S(1)} %copy-done.7, ...), kind=kOutput, calls=%fused_computation.24 | convolution fusion | flops 632291328 | bytes 19129344 | tf_op jit(solution)/shard_map/ikd,dc->cik/dot_general | solution.py:38
  34.0 10.8 %fusion.13 = bf16[1,128,192,96]{1,3,2,0:T(8,128)(2,1)} fusion(f32[192,96]{1,0:T(8,128)S(1)} %get-tuple-element.6, f32[192,96,128]{2,1,0:T(8,128)S(1)} %fusion.16, bf16[128,128]{1,0:T(8,128)(2,1)S(1)} %copy-done.11, bf16[192,96,128]{2,1,0:T(8,128)(2,1)S(1)} %copy-done.2, f32[128]{0:T(128)S(1)} %copy-done.6, f32[128]{0:T(128)S(1)} %copy-done.7, ...), kind=kOutput, calls=%fused_computation.25 | convolution fusion | flops 632291328 | bytes 19129344 | tf_op jit(solution)/shard_map/ikd,dc->cik/dot_general | solution.py:38
  44.8 8.2 %pad_maximum_fusion = bf16[2,128,192,96]{1,3,2,0:T(8,128)(2,1)} fusion(bf16[1,128,192,96]{1,3,2,0:T(8,128)(2,1)} %fusion.13, bf16[1,128,192,96]{1,3,2,0:T(8,128)(2,1)} %fusion.12), kind=kLoop, calls=%fused_computation.14 | loop fusion | flops 4718592 | bytes 18874368 | tf_op jit(solution)/shard_map/stack | solution.py:42
  53.0 15.7 %copy.50 = bf16[2,128,192,96]{3,2,0,1:T(8,128)(2,1)} copy(bf16[2,128,192,96]{1,3,2,0:T(8,128)(2,1)} %pad_maximum_fusion) | data formatting | bytes 18874368 | tf_op jit(solution)/shard_map/stack | solution.py:42
  68.7 146.6 %all_to_all.54 = bf16[2,128,192,96]{3,2,0,1:T(8,128)(2,1)} all-to-all(bf16[2,128,192,96]{3,2,0,1:T(8,128)(2,1)} %copy.50), channel_id=1, replica_groups=mesh['row'=8,'col'=16] {'row'}, dimensions={1} | all-to-all | bytes 18874368 | tf_op jit(solution)/shard_map/all_to_all | solution.py:44
  215.3 17.6 %copy.65 = bf16[2,16,8,192,96]{3,2,4,0,1:T(8,128)(2,1)} copy(bf16[2,16,8,192,96]{4,3,0,1,2:T(8,128)(2,1)} %bitcast.74) | data formatting | bytes 18874368 | tf_op jit(solution)/shard_map/all_to_all | solution.py:44
  232.9 19.9 %reshape.92 = bf16[2,16,1536,96]{2,3,0,1:T(8,128)(2,1)} reshape(bf16[2,16,8,192,96]{3,2,4,0,1:T(8,128)(2,1)} %copy.65) | data formatting | bytes 18874368 | tf_op jit(solution)/shard_map/all_to_all | solution.py:44
  252.8 115.8 %all_to_all.55 = bf16[2,16,1536,96]{2,3,0,1:T(8,128)(2,1)} all-to-all(bf16[2,16,1536,96]{2,3,0,1:T(8,128)(2,1)} %reshape.92), channel_id=1, replica_groups=mesh['row'=8,'col'=16] {'col'}, dimensions={1} | all-to-all | bytes 18874368 | tf_op jit(solution)/shard_map/all_to_all | solution.py:43
  368.7 8.3 %copy.71 = bf16[2,16,1536,96]{2,3,1,0:T(8,128)(2,1)} copy(bf16[2,16,1536,96]{2,3,0,1:T(8,128)(2,1)} %all_to_all.55) | data formatting | bytes 18874368 | tf_op jit(solution)/shard_map/all_to_all | solution.py:43
  377.0 10.9 %fusion.11 = bf16[1,1536,1536]{2,1,0:T(8,128)(2,1)S(1)} fusion(bf16[2,1,1536,16,96]{2,4,3,1,0:T(8,128)(2,1)} %bitcast.78), kind=kOutput, calls=%fused_computation.21 | convolution fusion | flops 7250116608 | bytes 14155776 | tf_op jit(solution)/shard_map/cjk,cik->cji/dot_general | solution.py:50
  387.9 52.2 %copy.72 = bf16[1,1536,1536]{2,0,1:T(2,128)(2,1)} copy(bf16[1,1536,1536]{2,1,0:T(8,128)(2,1)S(1)} %fusion.11) | data formatting | bytes 9437184 | tf_op jit(solution)/shard_map/convert_element_type | solution.py:52
  440.1 0.6 broadcast.100
  440.7 31.9 %reduce.2 = bf16[1536,1536]{1,0:T(8,128)(2,1)} reduce(bf16[1536,1,1536]{2,1,0:T(2,128)(2,1)} %bitcast.75, bf16[]{:T(256)} %broadcast.100), dimensions={1}, to_apply=%bitcast.72.reduce_sub_computation | reduce | bytes 9437186
  472.6 11.8 %reshape.93 = bf16[16,2,73728]{2,1,0:T(2,128)(2,1)} reshape(bf16[1536,1536]{1,0:T(8,128)(2,1)} %reduce.2) | data formatting | bytes 9437184
  484.4 62.1 %all_to_all.56 = bf16[16,2,73728]{2,1,0:T(2,128)(2,1)} all-to-all(bf16[16,2,73728]{2,1,0:T(2,128)(2,1)} %reshape.93), channel_id=1, replica_groups=mesh['row'=8,'col'=16] {'col'}, dimensions={0} | all-to-all | bytes 9437184 | tf_op jit(solution)/shard_map/all_to_all | solution.py:53
  546.4 12.8 %reshape.94 = bf16[1536,1,1536]{2,1,0:T(2,128)(2,1)} reshape(bf16[16,2,73728]{2,1,0:T(2,128)(2,1)} %all_to_all.56) | data formatting | bytes 9437184
  559.3 7.2 copy.68
  566.5 8.7 %copy.56 = bf16[16,96,1536]{1,0,2:T(8,128)(2,1)} copy(bf16[16,96,1536]{2,1,0:T(8,128)(2,1)} %bitcast.77) | data formatting | bytes 9437184 | tf_op jit(solution)/shard_map/all_to_all | solution.py:53
  575.1 4.7 all-to-all-start.3
  579.9 10.0 %fusion.21 = f32[192,96,128]{2,1,0:T(8,128)} fusion(bf16[128,128]{1,0:T(8,128)(2,1)S(1)} %copy-done.5, bf16[192,96,128]{2,1,0:T(8,128)(2,1)} %param.12, f32[128]{0:T(128)S(1)} %copy-done.6, f32[128]{0:T(128)S(1)} %copy-done.7, f32[192,96]{1,0:T(8,128)S(1)} %get-tuple-element.5, f32[192,96]{1,0:T(8,128)S(1)} %broadcast_multiply_fusion.2), kind=kOutput, calls=%fused_computation.38 | convolution fusion | flops 618135552 | bytes 14337024 | tf_op jit(solution)/shard_map/ijc,cd->jid/dot_general | solution.py:63
  589.8 60.8 %all-to-all-done.3 = bf16[16,96,1536]{1,0,2:T(8,128)(2,1)} async-done(((bf16[16,96,1536]{1,0,2:T(8,128)(2,1)}), bf16[16,96,1536]{1,0,2:T(8,128)(2,1)}, u32[]{:S(2)}, u32[]{:S(2)}) %all-to-all-start.3) | async-done | bytes 4718624 | tf_op jit(solution)/shard_map/all_to_all | solution.py:54
  650.7 8.4 %copy.57 = bf16[16,96,1536]{2,1,0:T(8,128)(2,1)} copy(bf16[16,96,1536]{1,0,2:T(8,128)(2,1)} %all-to-all-done.3) | data formatting | bytes 9437184 | tf_op jit(solution)/shard_map/all_to_all | solution.py:54
  659.1 11.0 %reshape.84 = f32[16,96,8,192]{3,2,1,0:T(8,128)} reshape(bf16[16,96,1536]{2,1,0:T(8,128)(2,1)} %copy.57) | data formatting | bytes 14155776 | tf_op jit(solution)/shard_map/convert_element_type | solution.py:55
  670.1 5.8 bitcast_reduce_fusion
  675.9 2.3 copy-done.3
  678.2 1.6 multiply_reduce_fusion
  679.9 0.0 copy-start.8
  679.9 0.0 copy-start.9
  679.9 13.2 %copy.58 = f32[8,16,96,192]{3,2,1,0:T(8,128)} copy(f32[8,16,96,192]{3,0,2,1:T(8,128)} %bitcast.73) | data formatting | bytes 18874368 | tf_op jit(solution)/shard_map/convert_element_type | solution.py:55
  693.1 9.4 %fusion.3 = bf16[128,96,192]{2,1,0:T(8,128)(2,1)} fusion(f32[8,16,96,192]{3,2,1,0:T(8,128)} %copy.58, f32[128]{0:T(128)S(1)} %copy-done.8, f32[128]{0:T(128)S(1)} %copy-done.9, f32[96,192]{1,0:T(8,128)S(1)} %add_rsqrt_fusion, f32[96,192]{1,0:T(8,128)S(1)} %broadcast_multiply_fusion), kind=kLoop, calls=%fused_computation.4 | loop fusion | flops 11796480 | bytes 14304256 | tf_op jit(solution)/shard_map/convert_element_type | solution.py:61
  702.5 9.6 %copy.62 = bf16[128,96,192]{0,1,2:T(8,128)(2,1)} copy(bf16[128,96,192]{2,1,0:T(8,128)(2,1)} %fusion.3) | data formatting | bytes 9437184 | tf_op jit(solution)/shard_map/convert_element_type | solution.py:61
  712.0 0.0 copy-start.1
  712.0 7.7 %fusion.10 = bf16[96,192,128]{2,0,1:T(8,128)(2,1)S(1)} fusion(f32[192,96,128]{2,1,0:T(8,128)} %fusion.21, bf16[128,96,192]{0,1,2:T(8,128)(2,1)} %copy.62, bf16[128,128]{1,0:T(8,128)(2,1)S(1)} %copy-done.12), kind=kOutput, calls=%fused_computation.17 | convolution fusion | flops 615776256 | bytes 18907136 | tf_op jit(solution)/shard_map/cji,cd->jid/dot_general | solution.py:62
  719.7 4.0 copy.61
  (19 shorter events, 0.1 us)
Async XLA Ops:
  0.0 12.9 %copy-start = (bf16[128,128]{1,0:T(8,128)(2,1)S(1)}, bf16[128,128]{1,0:T(8,128)(2,1)}, u32[]{:S(2)}) copy-start(bf16[128,128]{1,0:T(8,128)(2,1)} %param.17) | copy-start | bytes 98308
  0.0 12.9 %copy-start.7 = (f32[128]{0:T(128)S(1)}, f32[128]{0:T(128)}, u32[]{:S(2)}) copy-start(f32[128]{0:T(128)} %param.14) | copy-start | bytes 1540
  0.0 12.9 %copy-start.6 = (f32[128]{0:T(128)S(1)}, f32[128]{0:T(128)}, u32[]{:S(2)}) copy-start(f32[128]{0:T(128)} %param.15) | copy-start | bytes 1540
  0.8 12.1 %copy-start.2 = (bf16[192,96,128]{2,1,0:T(8,128)(2,1)S(1)}, bf16[192,96,128]{2,1,0:T(8,128)(2,1)}, u32[]{:S(2)}) copy-start(bf16[192,96,128]{2,1,0:T(8,128)(2,1)} %param.12) | copy-start | bytes 14155780
  13.0 5.1 copy-start.4
  18.0 5.1 copy-start.10
  23.1 10.8 %copy-start.11 = (bf16[128,128]{1,0:T(8,128)(2,1)S(1)}, bf16[128,128]{1,0:T(8,128)(2,1)}, u32[]{:S(2)}) copy-start(bf16[128,128]{1,0:T(8,128)(2,1)} %param.18) | copy-start | bytes 98308
  566.5 13.4 %copy-start.5 = (bf16[128,128]{1,0:T(8,128)(2,1)S(1)}, bf16[128,128]{1,0:T(8,128)(2,1)}, u32[]{:S(2)}) copy-start(bf16[128,128]{1,0:T(8,128)(2,1)} %param.20) | copy-start | bytes 98308
  575.1 75.5 %all-to-all-start.3 = ((bf16[16,96,1536]{1,0,2:T(8,128)(2,1)}), bf16[16,96,1536]{1,0,2:T(8,128)(2,1)}, u32[]{:S(2)}, u32[]{:S(2)}) async-start(bf16[16,96,1536]{1,0,2:T(8,128)(2,1)} %copy.56), calls=%async_computation.3 | async-start | bytes 12582912 | tf_op jit(solution)/shard_map/all_to_all | solution.py:54
  670.0 8.2 %copy-start.3 = (f32[16,96,8,192]{3,2,1,0:T(8,128)S(1)}, f32[16,96,8,192]{3,2,1,0:T(8,128)}, u32[]{:S(2)}) copy-start(f32[16,96,8,192]{3,2,1,0:T(8,128)} %reshape.84) | copy-start | bytes 28311556
  679.9 13.2 %copy-start.8 = (f32[128]{0:T(128)S(1)}, f32[128]{0:T(128)}, u32[]{:S(2)}) copy-start(f32[128]{0:T(128)} %param.22) | copy-start | bytes 1540
  679.9 13.2 %copy-start.9 = (f32[128]{0:T(128)S(1)}, f32[128]{0:T(128)}, u32[]{:S(2)}) copy-start(f32[128]{0:T(128)} %param.21) | copy-start | bytes 1540
  702.4 9.6 %copy-start.12 = (bf16[128,128]{1,0:T(8,128)(2,1)S(1)}, bf16[128,128]{1,0:T(8,128)(2,1)}, u32[]{:S(2)}) copy-start(bf16[128,128]{1,0:T(8,128)(2,1)} %param.23) | copy-start | bytes 98308
  712.0 11.7 %copy-start.1 = (bf16[128,128]{1,0:T(8,128)(2,1)S(1)}, bf16[128,128]{1,0:T(8,128)(2,1)}, u32[]{:S(2)}) copy-start(bf16[128,128]{1,0:T(8,128)(2,1)} %param.17) | copy-start | bytes 98308
where the time goes:
time: 738 us; the launch traced here: 724 us
  blocking collectives  325 us (44%)
  local copies, waits for them, and re-layouts  203 us (28%)
  other arithmetic  69.6 us (9%)
  waiting for transfers between devices  60.8 us (8%)
  matrix products  60.3 us (8%)
    all_to_all x1, blocking collectives, on_device(): lax.all_to_all(stacked, 'row', split_axis=1, concat_axis=2, tiled=True)  147 us
    all_to_all x1, blocking collectives, on_device(): lax.all_to_all(lax.all_to_all(stacked, 'row', split_axis=1, concat_axis=2...  116 us
    all_to_all x1, blocking collectives, on_device(): lax.all_to_all(product, 'col', split_axis=1, concat_axis=0, tiled=True)  62.1 us
    all_to_all x1, waiting for transfers between devices, on_device(): lax.all_to_all(by_cols, 'row', split_axis=2, concat_axis=0, tiled=True)  60.8 us
    convert_element_type x1, local copies, waits for them, and re-layouts, on_device(): product = jnp.einsum('cjk,cik->cji', edges[1], edges[0], preferred_elemen...  52.2 us
    all_to_all x2, local copies, waits for them, and re-layouts, on_device(): lax.all_to_all(stacked, 'row', split_axis=1, concat_axis=2, tiled=True)  37.5 us
    unnamed x30, local copies, waits for them, and re-layouts  34.8 us
    unnamed x1, other arithmetic  31.9 us
  transfers between devices with their start and end apart: 1, of which 1 were waited for; matrix products, arithmetic and copies ran while one was open for 1% of the time, Pallas kernels for 0%

commit v1 on v0

v1 whole, which is shorter than its diff:
```python
import jax
import jax.numpy as jnp
from jax import lax
from jax.experimental import pallas as pl
from jax.experimental.pallas import tpu as pltpu
from jax.sharding import PartitionSpec as P

EPS = 1e-05
N_ROW, N_COL = 8, 16
N_DEV = N_ROW * N_COL
NI, NK, CH = 192, 96, 128
PARTS = 3
KP = NK // PARTS
HP = KP // 2
TP = KP + HP
F32, BF16 = jnp.float32, jnp.bfloat16
MESH = pl.DeviceIdType.MESH


def coords():
    row, col = lax.axis_index("row"), lax.axis_index("col")
    return (col // 8) * 2 + row % 2, row // 2, (col // 2) % 4, col % 2


def each_peer(fn):
    x, y, z, core = coords()
    first = (x * 16 + y * 4 + z) * 5 + core * 64

    def body(s, _):
        t = (s + first) % N_DEV

        @pl.when(t != 0)
        def _():
            px, py, pz, pc = (x + t % 4) % 4, (y + t // 4 % 4) % 4, (z + t // 16 % 4) % 4, (core + t // 64) % 2
            fn(py * 2 + px % 2, (px // 2) * 8 + pz * 2 + pc)

        return 0

    lax.fori_loop(0, N_DEV, body, 0)


def send_part(src, dst, part, send_sem, recv_sem):
    me = lax.axis_index("row") * N_COL + lax.axis_index("col")

    def send(row, col):
        pltpu.make_async_remote_copy(
            src_ref=src.at[part, row * N_COL + col],
            dst_ref=dst.at[part, me],
            send_sem=send_sem.at[part],
            recv_sem=recv_sem.at[part],
            device_id={"row": row, "col": col},
            device_id_type=MESH,
        ).start()

    each_peer(send)
    dst[part, me] = src[part, me]


def wait_part(ref, part, sem):
    whole = ref.at[part, pl.ds(0, N_DEV - 1)]
    pltpu.make_async_copy(whole, whole, sem.at[part]).wait()


def loop(n, body, unroll=1):
    lax.fori_loop(0, n, lambda i, c: (body(i), c)[1], 0, unroll=unroll)


def low_lanes(shape):
    return lax.broadcasted_iota(jnp.int32, shape, 1) < 64


def kernel(
    z_hbm, mask_i, mask_s, gain, bias, w_l, w_lg, w_r, w_rg, w_og, og_s, ob_s, w_o,
    out_hbm,
    zb, nb, n32, s32, wt, send_r, send_l, recv_r, recv_l, right_t, left, recv_t, ob,
    z_sem, out_sem, rs, rr, ls, lr, ts, tr,
):
    row, col = lax.axis_index("row"), lax.axis_index("col")
    barrier = pltpu.get_barrier_semaphore()
    for p in range(PARTS):
        pltpu.make_async_copy(z_hbm.at[:, pl.ds(p * KP, KP), :], zb.at[p], z_sem.at[p]).start()
    each_peer(
        lambda r, c: pl.semaphore_signal(barrier, inc=1, device_id={"row": r, "col": c}, device_id_type=MESH)
    )

    wt[0] = w_r[...].T
    wt[1] = (w_rg[...].astype(F32) * 0.5).astype(BF16).T
    wt[2] = w_l[...].T
    wt[3] = (w_lg[...].astype(F32) * 0.5).astype(BF16).T

    def normalise(p):
        def body(i):
            v = zb[p, pl.ds(i * 4, 4)].astype(F32).reshape(4 * KP, CH)
            mean = jnp.mean(v, axis=-1, keepdims=True)
            c = v - mean
            var = jnp.mean(c * c, axis=-1, keepdims=True)
            n32[pl.ds(pl.multiple_of(i * 4 * KP, 4 * KP), 4 * KP), :] = (
                c * lax.rsqrt(var + EPS) * gain[...] + bias[...]
            )

        loop(NI // 4, body)

        def main(t):
            nb[p, t] = n32[pl.ds(t, 128, stride=KP), :].astype(BF16)

        loop(KP, main)

        def extra(t):
            nb[p, KP + t, 0:64] = n32[pl.ds(128 * KP + t, 64, stride=KP), :].astype(BF16)
            nb[p, KP + t, 64:128] = n32[pl.ds(128 * KP + HP + t, 64, stride=KP), :].astype(BF16)

        loop(HP, extra)

    def project(p, which, send):
        weights = wt[2 * which : 2 * which + 2].reshape(2 * CH, CH)
        k0 = col * NK + p * KP
        lanes = mask_i[pl.ds(row, 1), :] * 0.5

        def mask(k):
            return mask_s[k0 + k].astype(F32)

        def pair(t, mask_a, mask_b):
            rhs = nb[p, pl.ds(t, 2)].reshape(256, CH)
            both = lax.dot_general(weights, rhs, (((1,), (1,)), ((), ())), preferred_element_type=F32)
            gated = (jnp.tanh(both[CH:]) + 1.0) * both[:CH]
            s32[pl.ds(t, CH, stride=TP), :] = gated[:, :128] * mask_a
            s32[pl.ds(t + 1, CH, stride=TP), :] = gated[:, 128:] * mask_b

        def main(i):
            t = i * 2
            pair(t, lanes[:, :128] * mask(t), lanes[:, :128] * mask(t + 1))

        loop(KP // 2, main)

        def extra(i):
            t = i * 2
            pair(
                KP + t,
                lanes[:, 128:256] * mask(t) + lanes[:, 256:] * mask(t + HP),
                lanes[:, 128:256] * mask(t + 1) + lanes[:, 256:] * mask(t + 1 + HP),
            )

        loop(HP // 2, extra)

        def pack(i):
            rows = s32[pl.ds(pl.multiple_of(i * 4 * TP, 4 * TP), 4 * TP), :]
            send[p, pl.ds(i * 4, 4)] = rows.astype(BF16).reshape(4, TP, 128)

        loop(CH // 4, pack)

    def gate(p):
        def body(i):
            t = i * 2
            v = nb[p, pl.ds(t, 2)].reshape(256, CH)
            g = jnp.dot(v, w_og[...], preferred_element_type=F32)
            nb[p, pl.ds(t, 2)] = (0.5 * jnp.tanh(0.5 * g) + 0.5).astype(BF16).reshape(2, 128, CH)

        loop(TP // 2, body)

    def halves(ref, p, y, q):
        a = ref[p, pl.ds((2 * y) * N_COL + q, 4), KP:TP, :].astype(F32).reshape(4 * HP, 128)
        b = ref[p, pl.ds((2 * y + 1) * N_COL + q, 4), KP:TP, :].astype(F32).reshape(4 * HP, 128)
        low = low_lanes(a.shape)
        h0 = jnp.where(low, a, pltpu.roll(b, 64, 1)).reshape(4, 1, HP, 128)
        h1 = jnp.where(low, pltpu.roll(a, 64, 1), b).reshape(4, 1, HP, 128)
        return jnp.concatenate([h0, h1], axis=1).reshape(4 * KP, 128).astype(BF16)

    def take_right(p):
        def body(i):
            y, q = i // 4, i % 4 * 4
            lane = pl.ds(pl.multiple_of(p * N_COL * KP + q * KP, 128), 128)

            def put(r, first, tile, size):
                for l in range(0, size, KP):
                    at = first + l
                    dest = (at % NK) // KP * (N_COL * KP) + (2 * r + at // NK) * KP
                    right_t[pl.ds(pl.multiple_of(dest, KP), KP), lane] = tile[l : l + KP]

            for r in (2 * y, 2 * y + 1):
                put(r, 0, recv_r[p, pl.ds(r * N_COL + q, 4), 0:KP, :].reshape(128, 128).T, 128)
            both = halves(recv_r, p, y, q).T
            put(2 * y, 128, both[:64], 64)
            put(2 * y + 1, 128, both[64:], 64)

        loop(16, body)

    def take_left(p):
        def body(i):
            y, q = i // 4, i % 4 * 4
            k = pl.ds(pl.multiple_of(p * N_COL * KP + q * KP, 128), 128)
            for x in range(2):
                left[y, k, x * 128 : (x + 1) * 128] = recv_l[
                    p, pl.ds((2 * y + x) * N_COL + q, 4), 0:KP, :
                ].reshape(128, 128)
            left[y, k, 256:384] = halves(recv_l, p, y, q)

        loop(16, body)

    def product(s):
        def body(y):
            rows = right_t[pl.ds(s * N_COL * KP, N_COL * KP), :]
            tri = jnp.dot(rows, left[y], preferred_element_type=F32)
            for x in range(2):
                send_r[s, pl.ds((2 * y + x) * N_COL, N_COL), 0:KP, :] = (
                    tri[:, x * 128 : (x + 1) * 128].astype(BF16).reshape(N_COL, KP, 128)
                )
            last = tri[:, 256:].reshape(N_COL, 2, HP, 128)
            a, b = last[:, 0].reshape(N_COL * HP, 128), last[:, 1].reshape(N_COL * HP, 128)
            low = low_lanes(a.shape)
            e0 = jnp.where(low, a, pltpu.roll(b, 64, 1)).astype(BF16)
            e1 = jnp.where(low, pltpu.roll(a, 64, 1), b).astype(BF16)
            send_r[s, pl.ds((2 * y) * N_COL, N_COL), KP:TP, :] = e0.reshape(N_COL, HP, 128)
            send_r[s, pl.ds((2 * y + 1) * N_COL, N_COL), KP:TP, :] = e1.reshape(N_COL, HP, 128)

        loop(4, body)

    def finish(s):
        slot = s % 2
        step = 8

        def norm(g):
            rows = pl.ds(pl.multiple_of(g * 16, 16), 16)

            def some(i):
                return recv_t[s, pl.ds(i * step, step), rows, :].astype(F32)

            zero = jnp.zeros((16, 128), F32)
            mean = lax.fori_loop(0, CH // step, lambda i, a: a + jnp.sum(some(i), axis=0), zero) / CH

            def square(i, a):
                c = some(i) - mean[None]
                return a + jnp.sum(c * c, axis=0)

            var = lax.fori_loop(0, CH // step, square, zero) / CH
            scale = lax.rsqrt(var + EPS)

            def put(i):
                c = some(i) - mean[None]
                for e in range(step):
                    ch = i * step + e
                    s32[pl.ds(pl.multiple_of(ch * TP + g * 16, 16), 16), :] = c[e] * scale * og_s[ch] + ob_s[ch]

            loop(CH // step, put)

        loop(TP // 16, norm)

        def tile(t):
            v = s32[pl.ds(t, CH, stride=TP), :].astype(BF16)
            proj = jnp.dot(v.T, w_o[...], preferred_element_type=F32)
            return (proj * nb[s, t].astype(F32)).astype(BF16)

        def main(t):
            ob[slot, t, 0:128] = tile(t)

        loop(KP, main)

        def extra(t):
            v = tile(KP + t)
            ob[slot, t, 128:192] = v[:64]
            ob[slot, t + HP, 128:192] = v[64:]

        loop(HP, extra)
        return pltpu.make_async_copy(ob.at[slot], out_hbm.at[pl.ds(s * KP, KP)], out_sem.at[slot])

    for p in range(PARTS):
        pltpu.make_async_copy(z_hbm.at[:, pl.ds(p * KP, KP), :], zb.at[p], z_sem.at[p]).wait()
        normalise(p)
        project(p, 0, send_r)
        if p == 0:
            pl.semaphore_wait(barrier, N_DEV - 1)
        send_part(send_r, recv_r, p, rs, rr)
    for p in range(PARTS):
        project(p, 1, send_l)
        send_part(send_l, recv_l, p, ls, lr)
    for p in range(PARTS):
        gate(p)
    for p in range(PARTS):
        wait_part(recv_r, p, rr)
        take_right(p)
    for p in range(PARTS):
        wait_part(send_r, p, rs)
    for p in range(PARTS):
        wait_part(recv_l, p, lr)
        take_left(p)
    for s in range(PARTS):
        product(s)
        send_part(send_r, recv_t, s, ts, tr)
    stores = []
    for s in range(PARTS):
        wait_part(recv_t, s, tr)
        if s >= 2:
            stores[s - 2].wait()
        stores.append(finish(s))
        stores[s].start()
    for s in range(max(0, PARTS - 2), PARTS):
        stores[s].wait()
    for p in range(PARTS):
        wait_part(send_l, p, ls)
        wait_part(send_r, p, ts)


def on_device(
    pair_rep, res_mask, norm_gain, norm_bias, w_left, w_left_gate, w_right, w_right_gate, w_out_gate,
    out_gain, out_bias, w_out,
):
    by_row = res_mask.astype(F32).reshape(N_ROW, NI)
    none = jnp.zeros((N_ROW, 64), F32)
    mask_i = jnp.concatenate([by_row, none, none, by_row[:, 128:]], axis=1)
    vmem = pl.BlockSpec(memory_space=pltpu.VMEM)
    smem = pl.BlockSpec(memory_space=pltpu.SMEM)
    hbm = pl.BlockSpec(memory_space=pl.ANY)
    dma = pltpu.SemaphoreType.DMA
    slots = pltpu.VMEM((PARTS, N_DEV, TP, 128), BF16)
    return pl.pallas_call(
        kernel,
        out_shape=jax.ShapeDtypeStruct((NK, NI, CH), BF16),
        in_specs=[hbm, vmem, smem] + [vmem] * 7 + [smem, smem, vmem],
        out_specs=hbm,
        scratch_shapes=[
            pltpu.VMEM((PARTS, NI, KP, CH), BF16),
            pltpu.VMEM((PARTS, TP, 128, CH), BF16),
            pltpu.VMEM((NI * KP, CH), F32),
            pltpu.VMEM((CH * TP, 128), F32),
            pltpu.VMEM((4, CH, CH), BF16),
            slots, slots, slots, slots,
            pltpu.VMEM((N_COL * NK, N_COL * NK), BF16),
            pltpu.VMEM((4, N_COL * NK, 2 * NI), BF16),
            slots,
            pltpu.VMEM((2, KP, NI, CH), BF16),
            dma((PARTS,)), dma((2,)),
            dma((PARTS,)), dma((PARTS,)), dma((PARTS,)), dma((PARTS,)), dma((PARTS,)), dma((PARTS,)),
        ],
        compiler_params=pltpu.CompilerParams(
            collective_id=0, has_side_effects=True, vmem_limit_bytes=60 << 20
        ),
        cost_estimate=pl.CostEstimate(flops=11 * 10**9, bytes_accessed=10**7, transcendentals=7 * 10**6),
    )(
        pair_rep, mask_i, res_mask, norm_gain[None], norm_bias[None], w_left, w_left_gate, w_right,
        w_right_gate, w_out_gate, out_gain, out_bias, w_out,
    )


def solution(mesh):
    placed = (P("row", "col", None), P(), P(), P(), P(), P(), P(), P(), P(), P(), P(), P())
    return jax.shard_map(
        on_device, mesh=mesh, in_specs=placed, out_specs=P("col", "row", None), check_vma=False
    )
```

time: 738 us -> 230 us (0.31); the launches traced: 724 us -> 230 us
  blocking collectives: 325 us -> 0 us
  Pallas kernels: 0 us -> 224 us
  local copies, waits for them, and re-layouts: 203 us -> 5 us
  other arithmetic: 69.6 us -> 1.37 us
  waiting for transfers between devices: 60.8 us -> 0 us
  matrix products: 60.3 us -> 0 us
    all_to_all x3 -> x0, blocking collectives: 325 us -> none  [the longest x1 147 us: on_device(): lax.all_to_all(stacked, 'row', split_axis=1, concat_axis=2, tiled=True)]
    pallas_call x0 -> x1, Pallas kernels: none -> 224 us  [on_device(): pl.pallas_call(kernel, out_shape=jax.ShapeDtypeStruct((NK, NI, CH), BF16)...]
    convert_element_type x5 -> x0, local copies, waits for them, and re-layouts: 90 us -> none  [the longest x1 52.2 us: on_device(): product = jnp.einsum('cjk,cik->cji', edges[1], edges[0], preferred_elemen...]
    all_to_all x5 -> x0, local copies, waits for them, and re-layouts: 62.9 us -> none  [the longest x2 37.5 us: on_device(): lax.all_to_all(stacked, 'row', split_axis=1, concat_axis=2, tiled=True)]
    all_to_all x1 -> x0, waiting for transfers between devices: 60.8 us -> none  [on_device(): lax.all_to_all(by_cols, 'row', split_axis=2, concat_axis=0, tiled=True)]
    dot_general x7 -> x0, matrix products: 60.3 us -> none  [the longest x2 21.6 us: project(): jnp.einsum('ikd,dc->cik', normed, w_value, preferred_element_type=jnp.flo...]
    unnamed x1 -> x0, other arithmetic: 31.9 us -> none
    unnamed x30 -> x1, local copies, waits for them, and re-layouts: 34.8 us -> 4.84 us
  transfers between devices with their start and end apart: 1 -> 0, of which waited for: 1 -> 0; matrix products, arithmetic and copies ran while one was open for 1% -> 0% of each run, Pallas kernels for 0% -> 0%
where the time goes in v1:
time: 230 us
  Pallas kernels  224 us (97%)
  local copies, waits for them, and re-layouts  5 us (2%)
    pallas_call x1, Pallas kernels, on_device(): pl.pallas_call(kernel, out_shape=jax.ShapeDtypeStruct((NK, NI, CH), BF16)...  224 us
    unnamed x1, local copies, waits for them, and re-layouts  4.84 us

profile of v1, /device:TPU:1, one launch (start us, length us, event | category | flops | bytes accessed | tf_op | source)
XLA Modules:
  0.0 230.1 jit_solution(9012115299192268923)
XLA Ops:
  0.0 0.1 pad.1.clone
  0.1 0.7 convert_element_type.3
  0.8 0.1 reshape.3
  0.9 0.7 pad_maximum_fusion.mask_i
  1.5 223.8 %shard_map.118 = bf16[96,192,128]{2,1,0:T(8,128)(2,1)} custom-call(bf16[192,96,128]{2,1,0:T(8,128)(2,1)} %z_hbm.1, f32[8,384]{1,0:T(8,128)} %pad_maximum_fusion.mask_i, s32[1536]{0:T(1024)} %mask_s.1, f32[1,128]{1,0:T(1,128)} %bitcast.2, f32[1,128]{1,0:T(1,128)} %bitcast.3, bf16[128,128]{1,0:T(8,128)(2,1)} %w_l.1, bf16[128,128]{1,0:T(8,128)(2,1)} %w_lg.1, ...), custom_call_target="tpu_custom_call" | custom-call | flops 11000000512 | bytes 10000000 | tf_op jit(solution)/shard_map/pallas_call | solution.py:314
  225.3 4.8 %copy.14 = bf16[96,192,128]{2,1,0:T(8,128)(2,1)} copy(bf16[96,192,128]{2,1,0:T(8,128)(2,1)} %shard_map.118) | data formatting | bytes 9437184
  (2 shorter events, 0.0 us)

commit v2 on v1

v2 whole, which is shorter than its diff:
```python
import jax
import jax.numpy as jnp
from jax import lax
from jax.experimental import pallas as pl
from jax.experimental.pallas import tpu as pltpu
from jax.sharding import PartitionSpec as P

EPS = 1e-05
N_ROW, N_COL = 8, 16
N_DEV = N_ROW * N_COL
NI, NK, CH = 192, 96, 128
PARTS = 3
IP = NI // PARTS
TP = NK // 2
F32, BF16 = jnp.float32, jnp.bfloat16
MESH = pl.DeviceIdType.MESH


def coords():
    row, col = lax.axis_index("row"), lax.axis_index("col")
    return (col // 8) * 2 + row % 2, row // 2, (col // 2) % 4, col % 2


def each_peer(fn):
    x, y, z, core = coords()
    first = (x * 16 + y * 4 + z) * 5 + core * 64

    def body(s, _):
        t = (s + first) % N_DEV

        @pl.when(t != 0)
        def _():
            px, py, pz, pc = (x + t % 4) % 4, (y + t // 4 % 4) % 4, (z + t // 16 % 4) % 4, (core + t // 64) % 2
            fn(py * 2 + px % 2, (px // 2) * 8 + pz * 2 + pc)

        return 0

    lax.fori_loop(0, N_DEV, body, 0)


def send_part(src, dst, part, send_sem, recv_sem):
    me = lax.axis_index("row") * N_COL + lax.axis_index("col")

    def send(row, col):
        pltpu.make_async_remote_copy(
            src_ref=src.at[part, row * N_COL + col],
            dst_ref=dst.at[part, me],
            send_sem=send_sem.at[part],
            recv_sem=recv_sem.at[part],
            device_id={"row": row, "col": col},
            device_id_type=MESH,
        ).start()

    each_peer(send)
    dst[part, me] = src[part, me]


def wait_part(ref, part, sem):
    whole = ref.at[part, pl.ds(0, N_DEV - 1)]
    pltpu.make_async_copy(whole, whole, sem.at[part]).wait()


def loop(n, body, unroll=1):
    lax.fori_loop(0, n, lambda i, c: (body(i), c)[1], 0, unroll=unroll)


def low_lanes(shape):
    return lax.broadcasted_iota(jnp.int32, shape, len(shape) - 1) < 64


def swap_halves(a, b):
    low = low_lanes(a.shape)
    return jnp.where(low, a, pltpu.roll(b, 64, 1)), jnp.where(low, pltpu.roll(a, 64, 1), b)


def kernel(
    z_hbm, mask_v, mask_s, gain, bias, w_l, w_lg, w_r, w_rg, w_og, og_s, ob_s, w_o,
    out_hbm,
    zb, nb, n32, s32, wt, send_r, send_l, recv_r, recv_l, right_t, left, recv_t, ob,
    z_sem, out_sem, rs, rr, ls, lr, ts, tr,
):
    row, col = lax.axis_index("row"), lax.axis_index("col")
    barrier = pltpu.get_barrier_semaphore()

    def load(p):
        return pltpu.make_async_copy(z_hbm.at[pl.ds(p * IP, IP)], zb.at[p], z_sem.at[p])

    for p in range(PARTS):
        load(p).start()
    each_peer(
        lambda r, c: pl.semaphore_signal(barrier, inc=1, device_id={"row": r, "col": c}, device_id_type=MESH)
    )

    wt[0] = w_r[...].T
    wt[1] = (w_rg[...].astype(F32) * 0.5).astype(BF16).T
    wt[2] = w_l[...].T
    wt[3] = (w_lg[...].astype(F32) * 0.5).astype(BF16).T

    def normalise(p):
        ones = jnp.ones((2 * CH, CH), BF16)

        def body(i):
            v = zb[p, pl.ds(i * 2, 2)].reshape(2 * NK, CH)
            mean = jnp.dot(v, ones[:CH], preferred_element_type=F32) * (1 / CH)
            c = v.astype(F32) - mean
            sq = c * c
            high = sq.astype(BF16)
            rest = (sq - high.astype(F32)).astype(BF16)
            var = jnp.dot(jnp.concatenate([high, rest], axis=1), ones, preferred_element_type=F32) * (1 / CH)
            n32[pl.ds(pl.multiple_of(i * 2 * NK, 2 * NK), 2 * NK), :] = c * lax.rsqrt(var + EPS) * gain[...] + bias[...]

        loop(IP // 2, body, 2)

        def tile(t):
            nb[p, t, 0:64] = n32[pl.ds(t, 64, stride=NK), :].astype(BF16)
            nb[p, t, 64:128] = n32[pl.ds(TP + t, 64, stride=NK), :].astype(BF16)

        loop(TP, tile, 4)

    def project(p, which, send):
        weights = wt[2 * which : 2 * which + 2].reshape(2 * CH, CH)
        group = 3 * row + p
        low = low_lanes((1, 128))
        m = mask_v[pl.ds(group // 2, 1), :].astype(F32) * 0.5
        other = pltpu.roll(m, 64, 1)
        first = jnp.where(group % 2 == 0, m, other)
        second = jnp.where(group % 2 == 0, other, m)
        lanes = jnp.where(low, first, second)

        def mask(t):
            k = col * NK + t
            return lanes * jnp.where(low, mask_s[k].astype(F32), mask_s[k + TP].astype(F32))

        def pair(i):
            t = i * 2
            rhs = nb[p, pl.ds(t, 2)].reshape(256, CH)
            both = lax.dot_general(weights, rhs, (((1,), (1,)), ((), ())), preferred_element_type=F32)
            gated = (jnp.tanh(both[CH:]) + 1.0) * both[:CH]
            s32[pl.ds(t, CH, stride=TP), :] = gated[:, :128] * mask(t)
            s32[pl.ds(t + 1, CH, stride=TP), :] = gated[:, 128:] * mask(t + 1)

        loop(TP // 2, pair, 2)

        def pack(i):
            rows = s32[pl.ds(pl.multiple_of(i * 4 * TP, 4 * TP), 4 * TP), :]
            send[p, pl.ds(i * 4, 4)] = rows.astype(BF16).reshape(4, TP, 128)

        loop(CH // 4, pack, 2)

    def gate(p):
        def body(i):
            t = i * 2
            v = nb[p, pl.ds(t, 2)].reshape(256, CH)
            g = jnp.dot(v, w_og[...], preferred_element_type=F32)
            nb[p, pl.ds(t, 2)] = (0.5 * jnp.tanh(0.5 * g) + 0.5).astype(BF16).reshape(2, 128, CH)

        loop(TP // 2, body, 2)

    def two_rows(ref, p, y, q):
        a = ref[p, pl.ds((2 * y) * N_COL + q, 4)].astype(F32).reshape(4 * TP, 128)
        b = ref[p, pl.ds((2 * y + 1) * N_COL + q, 4)].astype(F32).reshape(4 * TP, 128)
        h0, h1 = swap_halves(a, b)
        both = jnp.concatenate([h0.reshape(4, 1, TP, 128), h1.reshape(4, 1, TP, 128)], axis=1)
        return both.reshape(4 * NK, 128).astype(BF16)

    def take_right(p):
        def body(i):
            y, q = i // 4, i % 4 * 4
            tile = two_rows(recv_r, p, y, q).T
            lane = pl.ds(pl.multiple_of(q * NK, 128), 4 * NK)
            for x in range(2):
                at = pl.multiple_of((2 * y + x) * NI + p * IP, IP)
                right_t[pl.ds(at, IP), lane] = tile[x * 64 : (x + 1) * 64]

        loop(16, body)

    def take_left(p):
        def body(i):
            y, q = i // 4, i % 4 * 4
            left[y, pl.ds(pl.multiple_of(q * NK, 128), 4 * NK), :] = two_rows(recv_l, p, y, q)

        loop(16, body)

    def product(s):
        def body(i):
            y, h = i // 4 * 2, i % 4
            rows = right_t[pl.ds(pl.multiple_of(h * 384, 384), 384), :]
            cols = jnp.concatenate([left[y], left[y + 1]], axis=1)
            tri = jnp.dot(rows, cols, preferred_element_type=F32)
            for x in range(2):
                both = tri[:, x * 128 : (x + 1) * 128].reshape(4, 2, TP, 128)
                e = swap_halves(both[:, 0].reshape(4 * TP, 128), both[:, 1].reshape(4 * TP, 128))
                for r in range(2):
                    slot = (2 * (y + x) + r) * N_COL + h * 4
                    send_r[s, pl.ds(slot, 4)] = e[r].astype(BF16).reshape(4, TP, 128)

        loop(8, body)

    def finish(s):
        slot = s % 2
        step = 16

        def norm(g):
            rows = pl.ds(pl.multiple_of(g * 16, 16), 16)

            def some(i):
                return recv_t[s, pl.ds(i * step, step), rows, :].astype(F32)

            zero = jnp.zeros((16, 128), F32)
            mean = lax.fori_loop(0, CH // step, lambda i, a: a + jnp.sum(some(i), axis=0), zero) * (1 / CH)

            def square(i, a):
                c = some(i) - mean[None]
                return a + jnp.sum(c * c, axis=0)

            var = lax.fori_loop(0, CH // step, square, zero) * (1 / CH)
            scale = lax.rsqrt(var + EPS)

            def put(i):
                c = some(i) - mean[None]
                for e in range(step):
                    ch = i * step + e
                    s32[pl.ds(pl.multiple_of(ch * TP + g * 16, 16), 16), :] = c[e] * scale * og_s[ch] + ob_s[ch]

            loop(CH // step, put)

        loop(TP // 16, norm)

        def tile(t):
            v = s32[pl.ds(t, CH, stride=TP), :].astype(BF16)
            proj = jnp.dot(v.T, w_o[...], preferred_element_type=F32)
            out = (proj * nb[s, t].astype(F32)).astype(BF16)
            ob[slot, t] = out[:64]
            ob[slot, t + TP] = out[64:]

        loop(TP, tile, 4)

    def store(s):
        return pltpu.make_async_copy(ob.at[s % 2], out_hbm.at[:, pl.ds(s * IP, IP)], out_sem.at[s % 2])

    for p in range(PARTS):
        load(p).wait()
        normalise(p)
        project(p, 0, send_r)
        if p == 0:
            pl.semaphore_wait(barrier, N_DEV - 1)
        send_part(send_r, recv_r, p, rs, rr)
    for p in range(PARTS):
        project(p, 1, send_l)
        send_part(send_l, recv_l, p, ls, lr)
    for p in range(PARTS):
        gate(p)
    for p in range(PARTS):
        wait_part(recv_r, p, rr)
        take_right(p)
    for p in range(PARTS):
        wait_part(send_r, p, rs)
        wait_part(recv_l, p, lr)
        take_left(p)
        product(p)
        send_part(send_r, recv_t, p, ts, tr)
    for p in range(PARTS):
        wait_part(recv_t, p, tr)
        if p >= 2:
            store(p - 2).wait()
        finish(p)
        store(p).start()
    for p in range(max(0, PARTS - 2), PARTS):
        store(p).wait()
    for p in range(PARTS):
        wait_part(send_l, p, ls)
        wait_part(send_r, p, ts)


def on_device(
    pair_rep, res_mask, norm_gain, norm_bias, w_left, w_left_gate, w_right, w_right_gate, w_out_gate,
    out_gain, out_bias, w_out,
):
    vmem = pl.BlockSpec(memory_space=pltpu.VMEM)
    smem = pl.BlockSpec(memory_space=pltpu.SMEM)
    hbm = pl.BlockSpec(memory_space=pl.ANY)
    dma = pltpu.SemaphoreType.DMA
    slots = pltpu.VMEM((PARTS, N_DEV, TP, 128), BF16)
    return pl.pallas_call(
        kernel,
        out_shape=jax.ShapeDtypeStruct((NK, NI, CH), BF16),
        in_specs=[hbm, vmem, smem] + [vmem] * 7 + [smem, smem, vmem],
        out_specs=hbm,
        scratch_shapes=[
            pltpu.VMEM((PARTS, IP, NK, CH), BF16),
            pltpu.VMEM((PARTS, TP, 128, CH), BF16),
            pltpu.VMEM((IP * NK, CH), F32),
            pltpu.VMEM((CH * TP, 128), F32),
            pltpu.VMEM((4, CH, CH), BF16),
            slots, slots, slots, slots,
            pltpu.VMEM((N_COL * NK, N_COL * NK), BF16),
            pltpu.VMEM((4, N_COL * NK, 128), BF16),
            slots,
            pltpu.VMEM((2, NK, IP, CH), BF16),
            dma((PARTS,)), dma((2,)),
            dma((PARTS,)), dma((PARTS,)), dma((PARTS,)), dma((PARTS,)), dma((PARTS,)), dma((PARTS,)),
        ],
        compiler_params=pltpu.CompilerParams(
            collective_id=0, has_side_effects=True, vmem_limit_bytes=60 << 20
        ),
        cost_estimate=pl.CostEstimate(flops=11 * 10**9, bytes_accessed=10**7, transcendentals=7 * 10**6),
    )(
        pair_rep, res_mask.reshape(12, 128), res_mask, norm_gain[None], norm_bias[None], w_left, w_left_gate, w_right,
        w_right_gate, w_out_gate, out_gain, out_bias, w_out,
    )


def solution(mesh):
    placed = (P("row", "col", None), P(), P(), P(), P(), P(), P(), P(), P(), P(), P(), P())
    return jax.shard_map(
        on_device, mesh=mesh, in_specs=placed, out_specs=P("col", "row", None), check_vma=False
    )
```

time: 230 us -> 193 us (0.84)
  Pallas kernels: 224 us -> 188 us
    pallas_call x1, Pallas kernels: 224 us -> 188 us  [on_device(): pl.pallas_call(kernel, out_shape=jax.ShapeDtypeStruct((NK, NI, CH), BF16)...]
where the time goes in v2:
time: 193 us
  Pallas kernels  188 us (97%)
  local copies, waits for them, and re-layouts  4.84 us (3%)
    pallas_call x1, Pallas kernels, on_device(): pl.pallas_call(kernel, out_shape=jax.ShapeDtypeStruct((NK, NI, CH), BF16)...  188 us
    unnamed x1, local copies, waits for them, and re-layouts  4.84 us

profile of v2, /device:TPU:1, one launch (start us, length us, event | category | flops | bytes accessed | tf_op | source)
XLA Modules:
  0.0 192.8 jit_solution(12209766823172031732)
XLA Ops:
  0.0 188.0 %shard_map.118 = bf16[96,192,128]{2,1,0:T(8,128)(2,1)} custom-call(bf16[192,96,128]{2,1,0:T(8,128)(2,1)} %z_hbm.1, s32[12,128]{1,0:T(8,128)} %bitcast.3, s32[1536]{0:T(1024)} %mask_s.1, f32[1,128]{1,0:T(1,128)} %bitcast.4, f32[1,128]{1,0:T(1,128)} %bitcast.5, bf16[128,128]{1,0:T(8,128)(2,1)} %w_l.1, bf16[128,128]{1,0:T(8,128)(2,1)} %w_lg.1, ...), custom_call_target="tpu_custom_call" | custom-call | flops 11000000512 | bytes 10000000 | tf_op jit(solution)/shard_map/pallas_call | solution.py:284
  188.0 4.8 %copy.14 = bf16[96,192,128]{2,1,0:T(8,128)(2,1)} copy(bf16[96,192,128]{2,1,0:T(8,128)(2,1)} %shard_map.118) | data formatting | bytes 9437184

commit v3 on v2

--- a/solution.py
+++ b/solution.py
@@ -21,42 +21,40 @@
     return (col // 8) * 2 + row % 2, row // 2, (col // 2) % 4, col % 2
 
 
-def each_peer(fn):
+def each_peer(fn, unroll=1):
     x, y, z, core = coords()
-    first = (x * 16 + y * 4 + z) * 5 + core * 64
+    first = ((x * 16 + y * 4 + z) * 5 + core * 64) % (N_DEV - 1)
 
     def body(s, _):
-        t = (s + first) % N_DEV
-
-        @pl.when(t != 0)
-        def _():
-            px, py, pz, pc = (x + t % 4) % 4, (y + t // 4 % 4) % 4, (z + t // 16 % 4) % 4, (core + t // 64) % 2
-            fn(py * 2 + px % 2, (px // 2) * 8 + pz * 2 + pc)
-
+        t = s + first
+        t = jnp.where(t >= N_DEV - 1, t - (N_DEV - 2), t + 1)
+        px, py, pz, pc = (x + t) & 3, (y + (t >> 2)) & 3, (z + (t >> 4)) & 3, (core + (t >> 6)) & 1
+        fn(py * 2 + (px & 1), (px >> 1) * 8 + pz * 2 + pc)
         return 0
 
-    lax.fori_loop(0, N_DEV, body, 0)
-
-
-def send_part(src, dst, part, send_sem, recv_sem):
+    lax.fori_loop(0, N_DEV - 1, body, 0, unroll=unroll)
+
+
+def send_part(src, dst, part, send_sem, recv_sem, start=0, size=TP, unroll=1):
     me = lax.axis_index("row") * N_COL + lax.axis_index("col")
+    rows = pl.ds(start, size)
 
     def send(row, col):
         pltpu.make_async_remote_copy(
-            src_ref=src.at[part, row * N_COL + col],
-            dst_ref=dst.at[part, me],
+            src_ref=src.at[part, row * N_COL + col, rows],
+            dst_ref=dst.at[part, me, rows],
             send_sem=send_sem.at[part],
             recv_sem=recv_sem.at[part],
             device_id={"row": row, "col": col},
             device_id_type=MESH,
         ).start()
 
-    each_peer(send)
-    dst[part, me] = src[part, me]
-
-
-def wait_part(ref, part, sem):
-    whole = ref.at[part, pl.ds(0, N_DEV - 1)]
+    each_peer(send, unroll)
+    dst[part, me, rows] = src[part, me, rows]
+
+
+def wait_part(ref, part, sem, start=0, size=TP):
+    whole = ref.at[part, pl.ds(0, N_DEV - 1), pl.ds(start, size)]
     pltpu.make_async_copy(whole, whole, sem.at[part]).wait()
 
 
@@ -77,7 +75,7 @@
     z_hbm, mask_v, mask_s, gain, bias, w_l, w_lg, w_r, w_rg, w_og, og_s, ob_s, w_o,
     out_hbm,
     zb, nb, n32, s32, wt, send_r, send_l, recv_r, recv_l, right_t, left, recv_t, ob,
-    z_sem, out_sem, rs, rr, ls, lr, ts, tr,
+    z_sem, out_sem, rs, rr, ls, lr, ts, tr, tr2,
 ):
     row, col = lax.axis_index("row"), lax.axis_index("col")
     barrier = pltpu.get_barrier_semaphore()
@@ -88,7 +86,7 @@
     for p in range(PARTS):
         load(p).start()
     each_peer(
-        lambda r, c: pl.semaphore_signal(barrier, inc=1, device_id={"row": r, "col": c}, device_id_type=MESH)
+        lambda r, c: pl.semaphore_signal(barrier, inc=1, device_id={"row": r, "col": c}, device_id_type=MESH), 4
     )
 
     wt[0] = w_r[...].T
@@ -96,28 +94,40 @@
     wt[2] = w_l[...].T
     wt[3] = (w_lg[...].astype(F32) * 0.5).astype(BF16).T
 
-    def normalise(p):
-        ones = jnp.ones((2 * CH, CH), BF16)
-
-        def body(i):
-            v = zb[p, pl.ds(i * 2, 2)].reshape(2 * NK, CH)
-            mean = jnp.dot(v, ones[:CH], preferred_element_type=F32) * (1 / CH)
-            c = v.astype(F32) - mean
-            sq = c * c
-            high = sq.astype(BF16)
-            rest = (sq - high.astype(F32)).astype(BF16)
-            var = jnp.dot(jnp.concatenate([high, rest], axis=1), ones, preferred_element_type=F32) * (1 / CH)
-            n32[pl.ds(pl.multiple_of(i * 2 * NK, 2 * NK), 2 * NK), :] = c * lax.rsqrt(var + EPS) * gain[...] + bias[...]
-
-        loop(IP // 2, body, 2)
+    def normed(v):
+        v = v.astype(F32)
+        mean = jnp.mean(v, axis=-1, keepdims=True)
+        c = v - mean
+        var = jnp.mean(c * c, axis=-1, keepdims=True)
+        return c * lax.rsqrt(var + EPS) * gain[...] + bias[...]
+
+    def normalise(p, start=0, size=TP):
+        if size == TP:
+
+            def body(i):
+                v = zb[p, pl.ds(i * 2, 2)].reshape(2 * NK, CH)
+                n32[pl.ds(pl.multiple_of(i * 2 * NK, 2 * NK), 2 * NK), :] = normed(v)
+
+            loop(IP // 2, body, 4)
+        else:
+
+            def body(i):
+                v = [zb[p, pl.ds(i * 4, 4), pl.ds(k, size)].reshape(4 * size, CH) for k in (start, start + TP)]
+                n = normed(jnp.concatenate(v, axis=0)).reshape(8, size, CH)
+                for e in range(8):
+                    at = (i * 4 + e % 4) * NK + start + e // 4 * TP
+                    n32[pl.ds(pl.multiple_of(at, 8), size), :] = n[e]
+
+            loop(IP // 4, body, 4)
 
         def tile(t):
+            t = start + t
             nb[p, t, 0:64] = n32[pl.ds(t, 64, stride=NK), :].astype(BF16)
             nb[p, t, 64:128] = n32[pl.ds(TP + t, 64, stride=NK), :].astype(BF16)
 
-        loop(TP, tile, 4)
-
-    def project(p, which, send):
+        loop(size, tile, 4)
+
+    def project(p, which, send, start=0, size=TP):
         weights = wt[2 * which : 2 * which + 2].reshape(2 * CH, CH)
         group = 3 * row + p
         low = low_lanes((1, 128))
@@ -132,18 +142,23 @@
             return lanes * jnp.where(low, mask_s[k].astype(F32), mask_s[k + TP].astype(F32))
 
         def pair(i):
-            t = i * 2
+            t = start + i * 2
             rhs = nb[p, pl.ds(t, 2)].reshape(256, CH)
             both = lax.dot_general(weights, rhs, (((1,), (1,)), ((), ())), preferred_element_type=F32)
             gated = (jnp.tanh(both[CH:]) + 1.0) * both[:CH]
             s32[pl.ds(t, CH, stride=TP), :] = gated[:, :128] * mask(t)
             s32[pl.ds(t + 1, CH, stride=TP), :] = gated[:, 128:] * mask(t + 1)
 
-        loop(TP // 2, pair, 2)
+        loop(size // 2, pair, 2)
 
         def pack(i):
-            rows = s32[pl.ds(pl.multiple_of(i * 4 * TP, 4 * TP), 4 * TP), :]
-            send[p, pl.ds(i * 4, 4)] = rows.astype(BF16).reshape(4, TP, 128)
+            if size == TP:
+                rows = s32[pl.ds(pl.multiple_of(i * 4 * TP, 4 * TP), 4 * TP), :]
+                send[p, pl.ds(i * 4, 4)] = rows.astype(BF16).reshape(4, TP, 128)
+            else:
+                for e in range(4):
+                    rows = s32[pl.ds(pl.multiple_of((i * 4 + e) * TP + start, 16), size), :]
+                    send[p, i * 4 + e, start : start + size] = rows.astype(BF16)
 
         loop(CH // 4, pack, 2)
 
@@ -196,12 +211,13 @@
 
         loop(8, body)
 
-    def finish(s):
+    def finish(s, start=0, size=TP):
         slot = s % 2
         step = 16
 
         def norm(g):
-            rows = pl.ds(pl.multiple_of(g * 16, 16), 16)
+            at = pl.multiple_of(start + g * 16, 16)
+            rows = pl.ds(at, 16)
 
             def some(i):
                 return recv_t[s, pl.ds(i * step, step), rows, :].astype(F32)
@@ -220,30 +236,36 @@
                 c = some(i) - mean[None]
                 for e in range(step):
                     ch = i * step + e
-                    s32[pl.ds(pl.multiple_of(ch * TP + g * 16, 16), 16), :] = c[e] * scale * og_s[ch] + ob_s[ch]
+                    s32[pl.ds(pl.multiple_of(ch * TP + at, 16), 16), :] = c[e] * scale * og_s[ch] + ob_s[ch]
 
             loop(CH // step, put)
 
-        loop(TP // 16, norm)
-
-        def tile(t):
+        loop(size // 16, norm)
+
+        def tile(i):
+            t = start + i
             v = s32[pl.ds(t, CH, stride=TP), :].astype(BF16)
             proj = jnp.dot(v.T, w_o[...], preferred_element_type=F32)
             out = (proj * nb[s, t].astype(F32)).astype(BF16)
             ob[slot, t] = out[:64]
             ob[slot, t + TP] = out[64:]
 
-        loop(TP, tile, 4)
+        loop(size, tile, 4)
 
     def store(s):
         return pltpu.make_async_copy(ob.at[s % 2], out_hbm.at[:, pl.ds(s * IP, IP)], out_sem.at[s % 2])
 
-    for p in range(PARTS):
+    load(0).wait()
+    for start, size in ((0, 16), (16, 32)):
+        normalise(0, start, size)
+        project(0, 0, send_r, start, size)
+        if start == 0:
+            pl.semaphore_wait(barrier, N_DEV - 1)
+        send_part(send_r, recv_r, 0, rs, rr, start, size, 4)
+    for p in range(1, PARTS):
         load(p).wait()
         normalise(p)
         project(p, 0, send_r)
-        if p == 0:
-            pl.semaphore_wait(barrier, N_DEV - 1)
         send_part(send_r, recv_r, p, rs, rr)
     for p in range(PARTS):
         project(p, 1, send_l)
@@ -253,23 +275,32 @@
     for p in range(PARTS):
         wait_part(recv_r, p, rr)
         take_right(p)
+    last = PARTS - 1
     for p in range(PARTS):
         wait_part(send_r, p, rs)
         wait_part(recv_l, p, lr)
         take_left(p)
         product(p)
-        send_part(send_r, recv_t, p, ts, tr)
-    for p in range(PARTS):
+        if p < last:
+            send_part(send_r, recv_t, p, ts, tr)
+        else:
+            send_part(send_r, recv_t, p, ts, tr, 0, 32)
+            send_part(send_r, recv_t, p, ts, tr2, 32, 16)
+    for p in range(last):
         wait_part(recv_t, p, tr)
-        if p >= 2:
-            store(p - 2).wait()
         finish(p)
         store(p).start()
-    for p in range(max(0, PARTS - 2), PARTS):
-        store(p).wait()
+    store(last - 2).wait()
+    wait_part(recv_t, last, tr, 0, 32)
+    finish(last, 0, 32)
+    wait_part(recv_t, last, tr2, 32, 16)
+    finish(last, 32, 16)
+    store(last).start()
     for p in range(PARTS):
         wait_part(send_l, p, ls)
         wait_part(send_r, p, ts)
+    store(last - 1).wait()
+    store(last).wait()
 
 
 def on_device(
@@ -298,7 +329,7 @@
             slots,
             pltpu.VMEM((2, NK, IP, CH), BF16),
             dma((PARTS,)), dma((2,)),
-            dma((PARTS,)), dma((PARTS,)), dma((PARTS,)), dma((PARTS,)), dma((PARTS,)), dma((PARTS,)),
+            dma((PARTS,)), dma((PARTS,)), dma((PARTS,)), dma((PARTS,)), dma((PARTS,)), dma((PARTS,)), dma((PARTS,)),
         ],
         compiler_params=pltpu.CompilerParams(
             collective_id=0, has_side_effects=True, vmem_limit_bytes=60 << 20

time: 193 us -> 178 us (0.922)
  Pallas kernels: 188 us -> 173 us
    pallas_call x1, Pallas kernels: 188 us -> 173 us  [on_device(): pl.pallas_call(kernel, out_shape=jax.ShapeDtypeStruct((NK, NI, CH), BF16)...]
where the time goes in v3:
time: 178 us
  Pallas kernels  173 us (97%)
  local copies, waits for them, and re-layouts  4.84 us (3%)
    pallas_call x1, Pallas kernels, on_device(): pl.pallas_call(kernel, out_shape=jax.ShapeDtypeStruct((NK, NI, CH), BF16)...  173 us
    unnamed x1, local copies, waits for them, and re-layouts  4.84 us

profile of v3, /device:TPU:1, one launch (start us, length us, event | category | flops | bytes accessed | tf_op | source)
XLA Modules:
  0.0 178.1 jit_solution(12070634433845117985)
XLA Ops:
  0.0 173.2 %shard_map.118 = bf16[96,192,128]{2,1,0:T(8,128)(2,1)} custom-call(bf16[192,96,128]{2,1,0:T(8,128)(2,1)} %z_hbm.1, s32[12,128]{1,0:T(8,128)} %bitcast.3, s32[1536]{0:T(1024)} %mask_s.1, f32[1,128]{1,0:T(1,128)} %bitcast.4, f32[1,128]{1,0:T(1,128)} %bitcast.5, bf16[128,128]{1,0:T(8,128)(2,1)} %w_l.1, bf16[128,128]{1,0:T(8,128)(2,1)} %w_lg.1, ...), custom_call_target="tpu_custom_call" | custom-call | flops 11000000512 | bytes 10000000 | tf_op jit(solution)/shard_map/pallas_call | solution.py:315
  173.2 4.8 %copy.14 = bf16[96,192,128]{2,1,0:T(8,128)(2,1)} copy(bf16[96,192,128]{2,1,0:T(8,128)(2,1)} %shard_map.118) | data formatting | bytes 9437184

commit v4 on v3

--- a/solution.py
+++ b/solution.py
@@ -72,10 +72,12 @@
 
 
 def kernel(
-    z_hbm, mask_v, mask_s, gain, bias, w_l, w_lg, w_r, w_rg, w_og, og_s, ob_s, w_o,
-    out_hbm,
-    zb, nb, n32, s32, wt, send_r, send_l, recv_r, recv_l, right_t, left, recv_t, ob,
-    z_sem, out_sem, rs, rr, ls, lr, ts, tr, tr2,
+    z_hbm, mask_v_hbm, mask_s_hbm, gain_hbm, bias_hbm, w_r_hbm, w_rg_hbm, w_l_hbm, w_lg_hbm, w_og_hbm, w_o_hbm,
+    og_hbm, ob_hbm,
+    out,
+    zb, nb, n32, s32, wt, send_r, send_l, recv_r, recv_l, right_t, left, recv_t,
+    mask_v, gain, bias, weights_in, mask_s, og_s, ob_s,
+    z_sem, in_sem, rs, rr, ls, lr, ts, tr, tr2,
 ):
     row, col = lax.axis_index("row"), lax.axis_index("col")
     barrier = pltpu.get_barrier_semaphore()
@@ -83,16 +85,23 @@
     def load(p):
         return pltpu.make_async_copy(z_hbm.at[pl.ds(p * IP, IP)], zb.at[p], z_sem.at[p])
 
-    for p in range(PARTS):
+    load(0).start()
+    small = [(gain_hbm, gain), (bias_hbm, bias), (mask_v_hbm, mask_v), (mask_s_hbm, mask_s), (og_hbm, og_s), (ob_hbm, ob_s)]
+    for i, ref in enumerate((w_r_hbm, w_rg_hbm, w_l_hbm, w_lg_hbm, w_og_hbm, w_o_hbm)):
+        small.append((ref, weights_in.at[i]))
+    small = [pltpu.make_async_copy(a, b, in_sem.at[i]) for i, (a, b) in enumerate(small)]
+    for copy in small:
+        copy.start()
+    for p in range(1, PARTS):
         load(p).start()
     each_peer(
-        lambda r, c: pl.semaphore_signal(barrier, inc=1, device_id={"row": r, "col": c}, device_id_type=MESH), 4
+        lambda r, c: pl.semaphore_signal(barrier, inc=1, device_id={"row": r, "col": c}, device_id_type=MESH), 16
     )
 
-    wt[0] = w_r[...].T
-    wt[1] = (w_rg[...].astype(F32) * 0.5).astype(BF16).T
-    wt[2] = w_l[...].T
-    wt[3] = (w_lg[...].astype(F32) * 0.5).astype(BF16).T
+    for copy in small:
+        copy.wait()
+    for i in range(4):
+        wt[i] = (weights_in[i].astype(F32) * (0.5 if i % 2 else 1.0)).astype(BF16).T
 
     def normed(v):
         v = v.astype(F32)
@@ -166,7 +175,7 @@
         def body(i):
             t = i * 2
             v = nb[p, pl.ds(t, 2)].reshape(256, CH)
-            g = jnp.dot(v, w_og[...], preferred_element_type=F32)
+            g = jnp.dot(v, weights_in[4], preferred_element_type=F32)
             nb[p, pl.ds(t, 2)] = (0.5 * jnp.tanh(0.5 * g) + 0.5).astype(BF16).reshape(2, 128, CH)
 
         loop(TP // 2, body, 2)
@@ -212,7 +221,6 @@
         loop(8, body)
 
     def finish(s, start=0, size=TP):
-        slot = s % 2
         step = 16
 
         def norm(g):
@@ -245,15 +253,12 @@
         def tile(i):
             t = start + i
             v = s32[pl.ds(t, CH, stride=TP), :].astype(BF16)
-            proj = jnp.dot(v.T, w_o[...], preferred_element_type=F32)
-            out = (proj * nb[s, t].astype(F32)).astype(BF16)
-            ob[slot, t] = out[:64]
-            ob[slot, t + TP] = out[64:]
+            proj = jnp.dot(v.T, weights_in[5], preferred_element_type=F32)
+            update = (proj * nb[s, t].astype(F32)).astype(BF16)
+            out[t, s * IP : (s + 1) * IP] = update[:64]
+            out[t + TP, s * IP : (s + 1) * IP] = update[64:]
 
         loop(size, tile, 4)
-
-    def store(s):
-        return pltpu.make_async_copy(ob.at[s % 2], out_hbm.at[:, pl.ds(s * IP, IP)], out_sem.at[s % 2])
 
     load(0).wait()
     for start, size in ((0, 16), (16, 32)):
@@ -289,18 +294,13 @@
     for p in range(last):
         wait_part(recv_t, p, tr)
         finish(p)
-        store(p).start()
-    store(last - 2).wait()
     wait_part(recv_t, last, tr, 0, 32)
     finish(last, 0, 32)
     wait_part(recv_t, last, tr2, 32, 16)
     finish(last, 32, 16)
-    store(last).start()
     for p in range(PARTS):
         wait_part(send_l, p, ls)
         wait_part(send_r, p, ts)
-    store(last - 1).wait()
-    store(last).wait()
 
 
 def on_device(
@@ -308,36 +308,41 @@
     out_gain, out_bias, w_out,
 ):
     vmem = pl.BlockSpec(memory_space=pltpu.VMEM)
-    smem = pl.BlockSpec(memory_space=pltpu.SMEM)
-    hbm = pl.BlockSpec(memory_space=pl.ANY)
+    hbm = pl.BlockSpec(memory_space=pltpu.HBM)
     dma = pltpu.SemaphoreType.DMA
     slots = pltpu.VMEM((PARTS, N_DEV, TP, 128), BF16)
     return pl.pallas_call(
         kernel,
-        out_shape=jax.ShapeDtypeStruct((NK, NI, CH), BF16),
-        in_specs=[hbm, vmem, smem] + [vmem] * 7 + [smem, smem, vmem],
-        out_specs=hbm,
+        out_shape=pltpu.VMEM((NK, NI, CH), BF16),
+        in_specs=[hbm] * 13,
+        out_specs=vmem,
         scratch_shapes=[
             pltpu.VMEM((PARTS, IP, NK, CH), BF16),
             pltpu.VMEM((PARTS, TP, 128, CH), BF16),
-            pltpu.VMEM((IP * NK, CH), F32),
-            pltpu.VMEM((CH * TP, 128), F32),
+            pltpu.VMEM((IP * NK + NK, CH), F32),
+            pltpu.VMEM((CH * TP + TP, 128), F32),
             pltpu.VMEM((4, CH, CH), BF16),
             slots, slots, slots, slots,
             pltpu.VMEM((N_COL * NK, N_COL * NK), BF16),
             pltpu.VMEM((4, N_COL * NK, 128), BF16),
             slots,
-            pltpu.VMEM((2, NK, IP, CH), BF16),
-            dma((PARTS,)), dma((2,)),
+            pltpu.VMEM((12, 128), jnp.int32),
+            pltpu.VMEM((1, CH), F32),
+            pltpu.VMEM((1, CH), F32),
+            pltpu.VMEM((6, CH, CH), BF16),
+            pltpu.SMEM((N_COL * NK,), jnp.int32),
+            pltpu.SMEM((CH,), F32),
+            pltpu.SMEM((CH,), F32),
+            dma((PARTS,)), dma((12,)),
             dma((PARTS,)), dma((PARTS,)), dma((PARTS,)), dma((PARTS,)), dma((PARTS,)), dma((PARTS,)), dma((PARTS,)),
         ],
         compiler_params=pltpu.CompilerParams(
-            collective_id=0, has_side_effects=True, vmem_limit_bytes=60 << 20
+            collective_id=0, has_side_effects=True, vmem_limit_bytes=58 << 20
         ),
         cost_estimate=pl.CostEstimate(flops=11 * 10**9, bytes_accessed=10**7, transcendentals=7 * 10**6),
     )(
-        pair_rep, res_mask.reshape(12, 128), res_mask, norm_gain[None], norm_bias[None], w_left, w_left_gate, w_right,
-        w_right_gate, w_out_gate, out_gain, out_bias, w_out,
+        pair_rep, res_mask.reshape(12, 128), res_mask, norm_gain[None], norm_bias[None], w_right, w_right_gate, w_left,
+        w_left_gate, w_out_gate, w_out, out_gain, out_bias,
     )
 
 

time: 178 us -> 174 us (0.978)
  local copies, waits for them, and re-layouts: 4.84 us -> 2.19 us
  Pallas kernels: 173 us -> 171 us
    unnamed x1, local copies, waits for them, and re-layouts: 4.84 us -> 2.19 us
    pallas_call x1, Pallas kernels: 173 us -> 171 us  [on_device(): pl.pallas_call(kernel, out_shape=pltpu.VMEM((NK, NI, CH), BF16), in_specs...]
where the time goes in v4:
time: 174 us; the launch traced here: 173 us
  Pallas kernels  171 us (98%)
  local copies, waits for them, and re-layouts  2.19 us (1%)
    pallas_call x1, Pallas kernels, on_device(): pl.pallas_call(kernel, out_shape=pltpu.VMEM((NK, NI, CH), BF16), in_specs...  171 us

profile of v4, /device:TPU:1, one launch (start us, length us, event | category | flops | bytes accessed | tf_op | source)
XLA Modules:
  0.0 173.4 jit_solution(6524363433051726685)
XLA Ops:
  0.0 171.2 %shard_map.118 = bf16[96,192,128]{2,1,0:T(8,128)(2,1)S(1)} custom-call(bf16[192,96,128]{2,1,0:T(8,128)(2,1)} %z_hbm.1, s32[12,128]{1,0:T(8,128)} %bitcast.3, s32[1536]{0:T(1024)} %mask_s_hbm.1, f32[1,128]{1,0:T(1,128)} %bitcast.4, f32[1,128]{1,0:T(1,128)} %bitcast.5, bf16[128,128]{1,0:T(8,128)(2,1)} %w_r_hbm.1, bf16[128,128]{1,0:T(8,128)(2,1)} %w_rg_hbm.1, ...), custom_call_target="tpu_custom_call" | custom-call | flops 11000000512 | bytes 10000000 | tf_op jit(solution)/shard_map/pallas_call | solution.py:314
  171.2 2.2 %copy.14 = bf16[96,192,128]{2,1,0:T(8,128)(2,1)} copy(bf16[96,192,128]{2,1,0:T(8,128)(2,1)S(1)} %shard_map.118) | data formatting | bytes 9437184

commit v5 on v4

--- a/solution.py
+++ b/solution.py
@@ -158,7 +158,7 @@
             s32[pl.ds(t, CH, stride=TP), :] = gated[:, :128] * mask(t)
             s32[pl.ds(t + 1, CH, stride=TP), :] = gated[:, 128:] * mask(t + 1)
 
-        loop(size // 2, pair, 2)
+        loop(size // 2, pair, 4)
 
         def pack(i):
             if size == TP:
@@ -258,7 +258,7 @@
             out[t, s * IP : (s + 1) * IP] = update[:64]
             out[t + TP, s * IP : (s + 1) * IP] = update[64:]
 
-        loop(size, tile, 4)
+        loop(size, tile, 16)
 
     load(0).wait()
     for start, size in ((0, 16), (16, 32)):

time: 174 us -> 172 us (0.989)
  no operation moved by 1% of the time
where the time goes in v5:
time: 172 us
  Pallas kernels  170 us (99%)
  local copies, waits for them, and re-layouts  2.19 us (1%)
    pallas_call x1, Pallas kernels, on_device(): pl.pallas_call(kernel, out_shape=pltpu.VMEM((NK, NI, CH), BF16), in_specs...  170 us

profile of v5, /device:TPU:1, one launch (start us, length us, event | category | flops | bytes accessed | tf_op | source)
XLA Modules:
  0.0 171.8 jit_solution(3587570537871042573)
XLA Ops:
  0.0 169.6 %shard_map.118 = bf16[96,192,128]{2,1,0:T(8,128)(2,1)S(1)} custom-call(bf16[192,96,128]{2,1,0:T(8,128)(2,1)} %z_hbm.1, s32[12,128]{1,0:T(8,128)} %bitcast.3, s32[1536]{0:T(1024)} %mask_s_hbm.1, f32[1,128]{1,0:T(1,128)} %bitcast.4, f32[1,128]{1,0:T(1,128)} %bitcast.5, bf16[128,128]{1,0:T(8,128)(2,1)} %w_r_hbm.1, bf16[128,128]{1,0:T(8,128)(2,1)} %w_rg_hbm.1, ...), custom_call_target="tpu_custom_call" | custom-call | flops 11000000512 | bytes 10000000 | tf_op jit(solution)/shard_map/pallas_call | solution.py:314
  169.6 2.2 %copy.14 = bf16[96,192,128]{2,1,0:T(8,128)(2,1)} copy(bf16[96,192,128]{2,1,0:T(8,128)(2,1)S(1)} %shard_map.118) | data formatting | bytes 9437184

commit v6 on v5

--- a/solution.py
+++ b/solution.py
@@ -169,7 +169,7 @@
                     rows = s32[pl.ds(pl.multiple_of((i * 4 + e) * TP + start, 16), size), :]
                     send[p, i * 4 + e, start : start + size] = rows.astype(BF16)
 
-        loop(CH // 4, pack, 2)
+        loop(CH // 4, pack, 4)
 
     def gate(p):
         def body(i):

time: 172 us -> 173 us (level)
  no operation moved by 1% of the time
where the time goes in v6:
time: 173 us; the launch traced here: 172 us
  Pallas kernels  170 us (98%)
  local copies, waits for them, and re-layouts  2.19 us (1%)
    pallas_call x1, Pallas kernels, on_device(): pl.pallas_call(kernel, out_shape=pltpu.VMEM((NK, NI, CH), BF16), in_specs...  170 us

profile of v6, /device:TPU:1, one launch (start us, length us, event | category | flops | bytes accessed | tf_op | source)
XLA Modules:
  0.0 171.8 jit_solution(17766848699101279558)
XLA Ops:
  0.0 169.6 %shard_map.118 = bf16[96,192,128]{2,1,0:T(8,128)(2,1)S(1)} custom-call(bf16[192,96,128]{2,1,0:T(8,128)(2,1)} %z_hbm.1, s32[12,128]{1,0:T(8,128)} %bitcast.3, s32[1536]{0:T(1024)} %mask_s_hbm.1, f32[1,128]{1,0:T(1,128)} %bitcast.4, f32[1,128]{1,0:T(1,128)} %bitcast.5, bf16[128,128]{1,0:T(8,128)(2,1)} %w_r_hbm.1, bf16[128,128]{1,0:T(8,128)(2,1)} %w_rg_hbm.1, ...), custom_call_target="tpu_custom_call" | custom-call | flops 11000000512 | bytes 10000000 | tf_op jit(solution)/shard_map/pallas_call | solution.py:314
  169.6 2.2 %copy.14 = bf16[96,192,128]{2,1,0:T(8,128)(2,1)} copy(bf16[96,192,128]{2,1,0:T(8,128)(2,1)S(1)} %shard_map.118) | data formatting | bytes 9437184
